TPU v7x, 32 devices: a whole 2x2x4 slice. The times are simulated.
32 devices in a mesh: sys: 2 (over y), row: 4 (over x, core), col: 4 (over z).
Axes of the slice: x: 2, y: 2, z: 4, core: 2. Of those that a mesh axis runs over, the one named last changes fastest.
Arguments:
- hamiltonian: bfloat16 [2048, 2048], P(('sys', 'row'), 'col'), parts along dimension 0, may hold values from -140 to 140
- row_ids: int32 [8, 4, 4], P(('sys', 'row'), 'col'), parts along dimension 0, may hold values from 0 to 7, as said below
- col_ids: int32 [8, 4, 8], P(('sys', 'row'), 'col'), parts along dimension 0, may hold values from 0 to 7, as said below
- counts: int32 [8, 4, 2], P(('sys', 'row'), 'col'), parts along dimension 0, may hold values from 2 to 8, as said below
Outputs:
- sign_estimate: bfloat16 [2048, 2048], P(('sys', 'row'), 'col'), parts along dimension 0
There are 2 independent parts, one for each index of `sys`. A program takes and returns all parts, laid end to end along the dimension named above; each array names one. Nothing has to cross between parts.
Inputs may be any that keep to these rules, and one draw needn't show every extreme that they name: `row_ids`: within a tile the 4 row ids are distinct. `col_ids`: within a tile the 8 column ids are distinct. counts[i, j, 0] is at most 4 and counts[i, j, 1] at most 8; one tile has both at their most.
All inputs are finite; a program needn't handle non-finite values.
Results may differ from a plain program's by a relative error of at most 0.0057.
Values may be sent and summed in bfloat16 or wider, within the bound.
A program may use at most 64 MiB of HBM per device.

v0:
```python
import jax
import jax.numpy as jnp
from jax import lax
from jax.sharding import PartitionSpec as P

BLK = 64
ACT = 8
RT = 4
CT = 8
NS_STEPS = 2


def shards(hamiltonian, row_ids, col_ids, counts):
    grid_rows = lax.axis_size("row")
    grid_cols = lax.axis_size("col")
    sub_panels = grid_rows // grid_cols
    my_row = lax.axis_index("row")
    my_col = lax.axis_index("col")
    tile_rows = hamiltonian.shape[0]
    tile_cols = hamiltonian.shape[1]
    every_rows, every_cols, every_counts = (
        lax.all_gather(row_ids, ("row", "col"), axis=0, tiled=True),
        lax.all_gather(col_ids, ("row", "col"), axis=0, tiled=True),
        lax.all_gather(counts, ("row", "col"), axis=0, tiled=True),
    )
    every_rows = every_rows.reshape(grid_rows, grid_cols, RT)
    every_cols = every_cols.reshape(grid_rows, grid_cols, CT)
    every_counts = every_counts.reshape(grid_rows, grid_cols, 2)
    row_live = jnp.arange(RT)[None, None, :] < every_counts[:, :, 0:1]
    col_live = jnp.arange(CT)[None, None, :] < every_counts[:, :, 1:2]
    global_rows = jnp.arange(grid_rows, dtype=jnp.int32)[:, None, None] * ACT + every_rows
    global_cols = (
        jnp.arange(grid_cols, dtype=jnp.int32)[None, :, None] * (sub_panels * ACT) + every_cols
    )
    own_rows = every_rows[my_row, my_col]
    own_cols = every_cols[my_row, my_col]
    own_row_live = row_live[my_row, my_col]
    own_col_live = col_live[my_row, my_col]
    block_mask = (
        jnp.repeat(own_row_live, BLK)[:, None] & jnp.repeat(own_col_live, BLK)[None, :]
    ).astype(jnp.float32)
    energy = hamiltonian.astype(jnp.float32) * block_mask
    total = lax.psum(jnp.sum(energy * energy), ("row", "col"))
    live_total = BLK * jnp.sum(every_counts[:, :, 0]).astype(jnp.float32)
    scale = 2.0 * jnp.sqrt(grid_cols * total / live_total + 1e-06)
    current = (energy / scale).astype(jnp.bfloat16)
    panel_rows = every_rows[my_row]
    row_match = (
        (panel_rows[:, None, :] == own_rows[None, :, None])
        & row_live[my_row][:, None, :]
        & own_row_live[None, :, None]
    )
    row_select = row_match.astype(jnp.bfloat16)
    pair_tile = jnp.arange(grid_rows, dtype=jnp.int32) // sub_panels
    left_cols = global_cols[my_row][pair_tile]
    left_live = col_live[my_row][pair_tile]
    right_rows = global_rows[:, my_col]
    right_live = row_live[:, my_col]
    matches = (
        (left_cols[:, None, :] == right_rows[:, :, None])
        & left_live[:, None, :]
        & right_live[:, :, None]
    )
    present_pairs = jnp.sum(matches.astype(jnp.int32), axis=2).reshape(-1)
    column_slot = (
        jnp.sum(jnp.where(matches, jnp.arange(CT, dtype=jnp.int32)[None, None, :], 0), axis=2)
        + pair_tile[:, None] * CT
    ).reshape(-1)
    col_match = (
        (every_cols[:, my_col][:, :, None] == own_cols[None, None, :])
        & col_live[:, my_col][:, :, None]
        & own_col_live[None, None, :]
    )
    col_tiles = col_match.astype(jnp.bfloat16)

    def multiply(left_full, right):
        left_blocks = left_full.reshape(tile_rows, grid_cols * CT, BLK)
        piece = lax.all_gather(right, "row", axis=0, tiled=True)
        piece_rows = piece.shape[0]
        tiles = piece_rows // tile_rows
        tile_index = jnp.arange(tiles, dtype=jnp.int32)
        selector = jnp.take(col_tiles, tile_index, axis=0)
        blocks = piece.reshape(tiles, tile_rows, CT, BLK)
        moved = jnp.einsum("tnxw,txc->tncw", blocks, selector, preferred_element_type=jnp.float32)
        moved = moved.astype(jnp.bfloat16).reshape(piece_rows, tile_cols)
        picked = jnp.take(left_blocks, column_slot, axis=1)
        picked = jnp.where(present_pairs[None, :, None] > 0, picked, jnp.zeros_like(picked))
        picked = picked.reshape(tile_rows, piece_rows)
        return jnp.dot(picked, moved, preferred_element_type=jnp.float32)

    final = None
    for sweep in range(NS_STEPS):
        arrange_blocks = lax.all_gather(current, "col", axis=1, tiled=True).reshape(
            RT, BLK, grid_cols, tile_cols
        )
        mapped = jnp.einsum(
            "mca,axmw->cxmw", row_select, arrange_blocks, preferred_element_type=jnp.float32
        )
        left_full = mapped.astype(jnp.bfloat16).reshape(tile_rows, grid_cols * tile_cols)
        square = multiply(left_full, current).astype(jnp.bfloat16)
        cube = multiply(left_full, square)
        update = 1.5 * current.astype(jnp.float32) - 0.5 * cube
        if sweep + 1 < NS_STEPS:
            current = update.astype(jnp.bfloat16)
        else:
            final = (update * scale).astype(jnp.bfloat16)
    return final


def solution(mesh):
    in_specs = (
        P(("sys", "row"), "col"),
        P(("sys", "row"), "col", None),
        P(("sys", "row"), "col", None),
        P(("sys", "row"), "col", None),
    )
    out_specs = P(("sys", "row"), "col")
    return jax.shard_map(shards, mesh=mesh, in_specs=in_specs, out_specs=out_specs, check_vma=False)
```

profile of v0, /device:TPU:0, one launch (start us, length us, event | category | flops | bytes accessed | tf_op | source)
XLA Modules:
  0.0 264.5 jit_solution(3802304550886430941)
XLA Ops:
  6.5 33.8 %all_gather.27 = s32[16,1,2]{2,1,0:T(1,128)S(1)} all-gather(s32[1,1,2]{2,1,0:T(1,128)} %param.11), channel_id=1, replica_groups=mesh['sys'=2,'row'=4,'col'=4] {'row','col'}, dimensions={0}, use_global_device_ids=true | all-gather | bytes 136 | tf_op jit(solution)/shard_map/all_gather | solution.py:24
  41.7 1.9 multiply_reduce_fusion
  43.5 30.4 %psum.7 = f32[]{:T(128)} all-reduce(f32[]{:T(128)} %multiply_reduce_fusion), channel_id=1, replica_groups=mesh['sys'=2,'row'=4,'col'=4] {'row','col'}, use_global_device_ids=true, to_apply=%region_1.0 | all-reduce | flops 1 | bytes 8 | tf_op jit(solution)/shard_map/psum | solution.py:43
  75.3 1.8 divide_convert_fusion
  78.0 30.8 %all_gather.29 = s32[16,1,4]{2,1,0:T(1,128)S(1)} all-gather(s32[1,1,4]{2,1,0:T(1,128)} %param.9), channel_id=1, replica_groups=mesh['sys'=2,'row'=4,'col'=4] {'row','col'}, dimensions={0}, use_global_device_ids=true | all-gather | bytes 272 | tf_op jit(solution)/shard_map/all_gather | solution.py:22
  109.0 28.5 %all_gather.28 = s32[16,1,8]{2,1,0:T(1,128)S(1)} all-gather(s32[1,1,8]{2,1,0:T(1,128)} %param.10), channel_id=1, replica_groups=mesh['sys'=2,'row'=4,'col'=4] {'row','col'}, dimensions={0}, use_global_device_ids=true | all-gather | bytes 544 | tf_op jit(solution)/shard_map/all_gather | solution.py:23
  140.2 1.8 reshape.101
  142.1 1.5 fusion
  143.6 1.6 copy.104
  145.2 1.4 reshape.167
  146.6 2.8 %reshape.168 = bf16[4,256,8,64]{3,2,1,0:T(8,128)(2,1)S(1)} reshape(bf16[1024,512]{1,0:T(8,128)(2,1)} %all-gather.9.cloned.1.call-done) | data formatting | bytes 2097152 | tf_op jit(solution)/shard_map/reshape | solution.py:83
  149.4 2.5 copy.80
  151.9 1.8 fusion.1
  156.2 1.2 convolution_convert_fusion.7
  157.7 15.3 %all-gather.11.cloned.1.call-done = bf16[1024,512]{1,0:T(8,128)(2,1)} async-done(((bf16[256,512]{1,0:T(8,128)(2,1)}), bf16[1024,512]{1,0:T(8,128)(2,1)}) %all-gather.11.cloned.1.call-update) | async-done | bytes 1048592 | tf_op jit(solution)/shard_map/all_gather | solution.py:78
  173.0 2.8 %reshape.169 = bf16[4,256,8,64]{3,2,1,0:T(8,128)(2,1)S(1)} reshape(bf16[1024,512]{1,0:T(8,128)(2,1)} %all-gather.11.cloned.1.call-done) | data formatting | bytes 2097152 | tf_op jit(solution)/shard_map/reshape | solution.py:83
  175.8 1.7 copy.84
  179.1 1.2 fusion.10
  181.0 27.5 %all-gather.13.cloned.1.call-done = bf16[256,2048]{1,0:T(8,128)(2,1)} async-done(((bf16[256,512]{1,0:T(8,128)(2,1)}), bf16[256,2048]{1,0:T(8,128)(2,1)}) %all-gather.13.cloned.1.call-update) | async-done | bytes 1048592 | tf_op jit(solution)/shard_map/all_gather | solution.py:93
  208.4 1.8 reshape.107
  210.3 1.5 fusion.3
  211.8 1.6 copy.113
  213.4 1.4 reshape.170
  215.4 1.0 bitcast_select_fusion
  216.3 9.8 %all-gather.15.cloned.1.call-done = bf16[1024,512]{1,0:T(8,128)(2,1)} async-done(((bf16[256,512]{1,0:T(8,128)(2,1)}), bf16[1024,512]{1,0:T(8,128)(2,1)}) %all-gather.15.cloned.1.call-update) | async-done | bytes 1048592 | tf_op jit(solution)/shard_map/all_gather | solution.py:78
  226.1 2.8 %reshape.171 = bf16[4,256,8,64]{3,2,1,0:T(8,128)(2,1)S(1)} reshape(bf16[1024,512]{1,0:T(8,128)(2,1)} %all-gather.15.cloned.1.call-done) | data formatting | bytes 2097152 | tf_op jit(solution)/shard_map/reshape | solution.py:83
  228.9 1.7 copy.91
  232.2 1.2 convolution_convert_fusion.6
  233.4 16.9 %all-gather.17.cloned.1.call-done = bf16[1024,512]{1,0:T(8,128)(2,1)} async-done(((bf16[256,512]{1,0:T(8,128)(2,1)}), bf16[1024,512]{1,0:T(8,128)(2,1)}) %all-gather.17.cloned.1.call-update) | async-done | bytes 1048592 | tf_op jit(solution)/shard_map/all_gather | solution.py:78
  250.3 2.8 %reshape.172 = bf16[4,256,8,64]{3,2,1,0:T(8,128)(2,1)S(1)} reshape(bf16[1024,512]{1,0:T(8,128)(2,1)} %all-gather.17.cloned.1.call-done) | data formatting | bytes 2097152 | tf_op jit(solution)/shard_map/reshape | solution.py:83
  253.1 1.7 copy.95
  256.5 1.2 fusion.9
  (82 shorter events, 13.8 us)
Async XLA Ops:
  6.5 133.7 %all-gather.7.cloned.1.call-start = ((), (), s32[]{:S(2)}) async-start(), calls=%async_computation | async-start | bytes 1310720 | tf_op jit(solution)/shard_map/all_gather | solution.py:93
  77.1 69.4 %all-gather.9.cloned.1.call-start = ((), (), s32[]{:S(2)}) async-start(), calls=%async_computation.1 | async-start | bytes 1310720 | tf_op jit(solution)/shard_map/all_gather | solution.py:78
  77.9 95.1 %all-gather.11.cloned.1.call-start = ((), (), s32[]{:S(2)}) async-start(), calls=%async_computation.2 | async-start | bytes 1310720 | tf_op jit(solution)/shard_map/all_gather | solution.py:78
  155.4 0.8 copy-start.3
  157.4 51.0 %all-gather.13.cloned.1.call-start = ((), (), s32[]{:S(2)}) async-start(), calls=%async_computation.3 | async-start | bytes 1310720 | tf_op jit(solution)/shard_map/all_gather | solution.py:93
  178.0 1.1 copy-start
  178.0 1.1 copy-start.4
  180.3 45.7 %all-gather.15.cloned.1.call-start = ((), (), s32[]{:S(2)}) async-start(), calls=%async_computation.4 | async-start | bytes 1310720 | tf_op jit(solution)/shard_map/all_gather | solution.py:78
  180.9 69.4 %all-gather.17.cloned.1.call-start = ((), (), s32[]{:S(2)}) async-start(), calls=%async_computation.5 | async-start | bytes 1310720 | tf_op jit(solution)/shard_map/all_gather | solution.py:78
  231.1 1.1 copy-start.1
  255.3 1.1 copy-start.2
  255.4 1.1 copy-start.5
Sparse Core Ops, SparseCore 0:
  77.3 26.9 all-gather.6
  105.8 16.2 all-gather.8
  157.6 15.3 all-gather.10
  180.5 27.9 all-gather.12
  209.8 16.2 all-gather.14
  233.5 16.7 all-gather.16
where the time goes:
time: 265 us; the launch traced here: 264 us
  blocking collectives  123 us (46%)
  waiting for transfers between devices  70.7 us (27%)
  local copies, waits for them, and re-layouts  37.3 us (14%)
  between operations  15.3 us (6%)
  matrix products  11.1 us (4%)
  other arithmetic  6.18 us (2%)
    all_gather x4, waiting for transfers between devices, multiply(): piece = lax.all_gather(right, 'row', axis=0, tiled=True)  42 us
    all_gather x1, blocking collectives, shards(): lax.all_gather(counts, ('row', 'col'), axis=0, tiled=True)  33.8 us
    all_gather x1, blocking collectives, shards(): lax.all_gather(row_ids, ('row', 'col'), axis=0, tiled=True)  30.8 us
    psum x1, blocking collectives, shards(): total = lax.psum(jnp.sum(energy * energy), ('row', 'col'))  30.4 us
    all_gather x1, blocking collectives, shards(): lax.all_gather(col_ids, ('row', 'col'), axis=0, tiled=True)  28.5 us
    all_gather x2, waiting for transfers between devices, shards(): lax.all_gather(current, 'col', axis=1, tiled=True)  27.5 us
    reshape x8, local copies, waits for them, and re-layouts, multiply(): blocks = piece.reshape(tiles, tile_rows, CT, BLK)  18.7 us
    another operation x4, local copies, waits for them, and re-layouts, multiply(): left_blocks = left_full.reshape(tile_rows, grid_cols * CT, BLK)  5.98 us
  transfers between devices with their start and end apart: 6, of which 4 were waited for; matrix products, arithmetic and copies ran while one was open for 6% of the time, Pallas kernels for 0%

commit v1 on v0

--- a/solution.py
+++ b/solution.py
@@ -1,6 +1,8 @@
 import jax
 import jax.numpy as jnp
 from jax import lax
+from jax.experimental import pallas as pl
+from jax.experimental.pallas import tpu as pltpu
 from jax.sharding import PartitionSpec as P
 
 BLK = 64
@@ -8,6 +10,290 @@
 RT = 4
 CT = 8
 NS_STEPS = 2
+
+LINE = 4
+ROWS = RT * BLK
+COLS = CT * BLK
+FULL = LINE * ROWS
+MESH_IDS = pl.DeviceIdType.MESH
+
+
+def onehot(found):
+    return jnp.where(found, 1.0, 0.0).astype(jnp.bfloat16)
+
+
+def dot(a, b):
+    return jnp.dot(a, b, preferred_element_type=jnp.float32)
+
+
+def lines_kernel(
+    h_ref, rid, cid, cnt, o_ref,
+    tiles, meta, down, left, right, picked, select, masks, half, whole, left2, square2,
+    send, recv, meta_send, meta_recv,
+):
+    k = lax.axis_index("row")
+    z = lax.axis_index("col")
+    ks = k + 1 - 2 * (k % 2)
+    kx = (k + 2) % LINE
+    kxs = (ks + 2) % LINE
+    barrier = pltpu.get_barrier_semaphore()
+    others = [(a, b) for a in range(LINE) for b in range(LINE) if a or b]
+    for a, b in others:
+        pl.semaphore_signal(
+            barrier, inc=1, device_id={"row": (k + a) % LINE, "col": (z + b) % LINE}, device_id_type=MESH_IDS
+        )
+    live_rows = cnt[0, 0, 0]
+    live_cols = cnt[0, 0, 1]
+
+    lane = lax.broadcasted_iota(jnp.int32, (BLK, COLS), 1)
+    sub = lax.broadcasted_iota(jnp.int32, (BLK, COLS), 0)
+    for c in range(CT):
+        offset = jnp.where(c < live_cols, cid[0, 0, c] * BLK, -COLS)
+        select[pl.ds(c * BLK, BLK), 0:COLS] = onehot(sub + offset == lane)
+    natural = dot(h_ref[...], select[:, 0:COLS])
+    energy = jnp.zeros((1, COLS), jnp.float32)
+    for r in range(RT):
+        part = natural[r * BLK:(r + 1) * BLK] * jnp.where(r < live_rows, 1.0, 0.0)
+        tiles[z, pl.ds(pl.multiple_of(k * ROWS + r * BLK, BLK), BLK), :] = part.astype(jnp.bfloat16)
+        energy += jnp.sum(part * part, axis=0, keepdims=True)
+    lane1 = lax.broadcasted_iota(jnp.int32, (1, COLS), 1)
+    block1 = lane1 // BLK
+    within = lane1 % BLK
+    row_full = jnp.full((1, COLS), -1, jnp.int32)
+    for r in range(RT):
+        row_full = jnp.where((block1 == r) & (r < live_rows), rid[0, 0, r] * BLK + within, row_full)
+    row_full = row_full.astype(jnp.float32)
+    col_mask = jnp.zeros((1, COLS), jnp.float32)
+    col_full = jnp.full((1, COLS), -1, jnp.int32)
+    for c in range(CT):
+        alive = c < live_cols
+        col_mask = jnp.where((block1 == cid[0, 0, c]) & alive, 1.0, col_mask)
+        col_full = jnp.where((block1 == c) & alive, cid[0, 0, c] * BLK + within, col_full)
+    own_meta = meta.at[k, z]
+    own_meta[0:1, :] = row_full[:, 0:128]
+    own_meta[1:2, :] = row_full[:, 128:256]
+    for q in range(4):
+        own_meta[2 + q:3 + q, :] = col_mask[:, q * 128:(q + 1) * 128]
+    own_meta[6:7, :] = energy[:, 0:128] + energy[:, 128:256] + energy[:, 256:384] + energy[:, 384:512]
+    own_meta[7:8, :] = jnp.full((1, 128), live_rows, jnp.int32).astype(jnp.float32)
+    pl.semaphore_wait(barrier, len(others))
+
+    def piece(kk, m):
+        return tiles.at[m, pl.ds(pl.multiple_of(kk * ROWS, ROWS), ROWS), :]
+
+    def copy(kind, kk, m, row, col):
+        return pltpu.make_async_remote_copy(
+            src_ref=piece(kk, m), dst_ref=piece(kk, m),
+            send_sem=send.at[kind, m], recv_sem=recv.at[kk, m],
+            device_id={"row": row, "col": col}, device_id_type=MESH_IDS,
+        )
+
+    def meta_copy(n, a, b):
+        return pltpu.make_async_remote_copy(
+            src_ref=meta.at[k, z], dst_ref=meta.at[k, z],
+            send_sem=meta_send.at[n], recv_sem=meta_recv.at[k, z],
+            device_id={"row": (k + a) % LINE, "col": (z + b) % LINE}, device_id_type=MESH_IDS,
+        )
+
+    def line_copies(m, act):
+        @pl.when((m <= z) & (z < LINE - 1))
+        def _():
+            act(copy(0, k, m, k, z + 1))
+
+        @pl.when((m >= z) & (z > 0))
+        def _():
+            act(copy(1, k, m, k, z - 1))
+
+        act(copy(2, k, m, kx, z))
+        act(copy(3, k, m, ks, z))
+
+    def start(c):
+        c.start()
+
+    def finish(c):
+        c.wait_send()
+
+    def arrived(kk, m):
+        copy(0, kk, m, ks, z).wait_recv()
+
+    high = z // 2
+    near = z * (1 - high) + (LINE - 1 - z) * high
+
+    def panel_at(t):
+        later = t // 2
+        m = 2 * later + (t + near * (1 - later)) % 2
+        return m * (1 - high) + (LINE - 1 - m) * high
+
+    line_copies(z, start)
+    for n, (a, b) in enumerate(others):
+        meta_copy(n, a, b).start()
+    for a, b in others:
+        row, col = (k + a) % LINE, (z + b) % LINE
+        pltpu.make_async_remote_copy(
+            src_ref=meta.at[row, col], dst_ref=meta.at[row, col],
+            send_sem=meta_send.at[0], recv_sem=meta_recv.at[row, col],
+            device_id={"row": row, "col": col}, device_id_type=MESH_IDS,
+        ).wait_recv()
+
+    def lane_ids(kk, m):
+        return jnp.concatenate([meta[kk, m, 0:1, :], meta[kk, m, 1:2, :]], axis=1)
+
+    def natural_mask(kk, m):
+        return jnp.concatenate([meta[kk, m, 2 + q:3 + q, :] for q in range(4)], axis=1)
+
+    for a in range(LINE):
+        for b in range(LINE):
+            for q in range(2):
+                wide = jnp.broadcast_to(meta[a, b, q:q + 1, :], (128, 128))
+                down[a, b, pl.ds(q * 128, 128), :] = wide.T
+
+    def row_select(kk, to, of):
+        ids = down[kk, to]
+        return onehot(jnp.concatenate([ids, ids], axis=1) == lane_ids(kk, of))
+
+    sub_wide = lax.broadcasted_iota(jnp.int32, (COLS, ROWS), 0).astype(jnp.float32)
+
+    def col_select(m, to):
+        return onehot(sub_wide == lane_ids(m, to))
+
+    def wide_slice(index):
+        return pl.ds(pl.multiple_of(index * ROWS, ROWS), ROWS)
+
+    def stage(t, carry):
+        @pl.when(t < LINE - 1)
+        def _():
+            m1 = panel_at(t + 1)
+            arrived(k, m1)
+            line_copies(m1, start)
+
+        m = panel_at(t)
+        arrived(kx, m)
+        copy(4, kx, m, ks, z).start()
+        for to in range(LINE):
+            select[:, pl.ds(to * ROWS, ROWS)] = col_select(m, to)
+        arrived(ks, m)
+        arrived(kxs, m)
+
+        def rows_of(kk, carry):
+            picked[...] = dot(tiles[m, wide_slice(kk), :], select[...]).astype(jnp.bfloat16)
+            right[m, wide_slice(kk), :] = picked[:, wide_slice(z)]
+            mask = jnp.broadcast_to(natural_mask(kk, m), (16, COLS)).astype(jnp.bfloat16)
+            masks[kk, m] = dot(mask, select[:, wide_slice(z)])
+            for to in range(LINE):
+                block = dot(row_select(kk, to, m), picked[:, pl.ds(to * ROWS, ROWS)])
+                left[to, wide_slice(kk), wide_slice(m)] = block.astype(jnp.bfloat16)
+            return carry
+
+        return lax.fori_loop(0, LINE, rows_of, carry)
+
+    lax.fori_loop(0, LINE, stage, 0)
+
+    total = jnp.zeros((1, 128), jnp.float32)
+    count = jnp.zeros((1, 128), jnp.float32)
+    for a in range(LINE):
+        for b in range(LINE):
+            total += meta[a, b, 6:7, :]
+            count += meta[a, b, 7:8, :]
+    total = jnp.sum(total, axis=1, keepdims=True)
+    count = jnp.max(count, axis=1, keepdims=True) * BLK
+    scale = 2.0 * jnp.sqrt(LINE * total / count + 1e-06)
+    lin = 1.5 / scale
+    cub = 0.5 / scale / scale / scale
+
+    def other(d, carry):
+        m = (z + d) % LINE
+
+        def square_rows(kk, carry):
+            part = dot(left[m, wide_slice(kk), :], right[m]) * masks[kk, m, 0:1, :]
+            half[wide_slice(kk), :] = part.astype(jnp.bfloat16)
+            return carry
+
+        lax.fori_loop(0, LINE, square_rows, 0)
+
+        def cube_rows(kk, carry):
+            part = dot(left[m, wide_slice(kk), :], half[...]) * masks[kk, m, 0:1, :]
+            new = lin * right[m, wide_slice(kk), :].astype(jnp.float32) - cub * part
+            moved = dot(row_select(kk, z, m), new.astype(jnp.bfloat16))
+            left2[wide_slice(kk), wide_slice(m)] = moved.astype(jnp.bfloat16)
+            return carry
+
+        return lax.fori_loop(0, LINE, cube_rows, carry)
+
+    lax.fori_loop(1, LINE, other, 0)
+
+    def own_square(kk, carry):
+        part = dot(left[z, wide_slice(kk), :], tiles[z]) * natural_mask(kk, z)
+        square2[wide_slice(kk), :] = part.astype(jnp.bfloat16)
+        return carry
+
+    lax.fori_loop(0, LINE, own_square, 0)
+    select[:, 0:ROWS] = col_select(z, z)
+
+    def own_cube(kk, carry):
+        part = dot(left[z, wide_slice(kk), :], square2[...]) * natural_mask(kk, z)
+        new = lin * tiles[z, wide_slice(kk), :].astype(jnp.float32) - cub * part
+        new = new.astype(jnp.bfloat16)
+        whole[wide_slice(kk), :] = new
+        left2[wide_slice(kk), wide_slice(z)] = dot(new, select[:, 0:ROWS]).astype(jnp.bfloat16)
+        return carry
+
+    lax.fori_loop(0, LINE, own_cube, 0)
+
+    def second_square(kk, carry):
+        part = dot(left2[wide_slice(kk), :], whole[...]) * natural_mask(kk, z)
+        square2[wide_slice(kk), :] = part.astype(jnp.bfloat16)
+        return carry
+
+    lax.fori_loop(0, LINE, second_square, 0)
+    cube = dot(left2[wide_slice(k), :], square2[...]) * natural_mask(k, z)
+    update = 1.5 * whole[wide_slice(k), :].astype(jnp.float32) - 0.5 * cube
+    final = (update * scale).astype(jnp.bfloat16)
+    back = onehot(lax.broadcasted_iota(jnp.int32, (COLS, COLS), 0) == col_full)
+    o_ref[...] = dot(final, back).astype(jnp.bfloat16)
+
+    for n, (a, b) in enumerate(others):
+        meta_copy(n, a, b).wait_send()
+
+    def drain(m, carry):
+        line_copies(m, finish)
+        copy(4, kx, m, ks, z).wait_send()
+        return carry
+
+    lax.fori_loop(0, LINE, drain, 0)
+
+
+def line_shards(hamiltonian, row_ids, col_ids, counts):
+    smem = pl.BlockSpec(memory_space=pltpu.SMEM)
+    vmem = pl.BlockSpec(memory_space=pltpu.VMEM)
+    bf16, f32 = jnp.bfloat16, jnp.float32
+    return pl.pallas_call(
+        lines_kernel,
+        out_shape=jax.ShapeDtypeStruct((ROWS, COLS), bf16),
+        in_specs=[vmem, smem, smem, smem],
+        out_specs=vmem,
+        scratch_shapes=[
+            pltpu.VMEM((LINE, FULL, COLS), bf16),
+            pltpu.VMEM((LINE, LINE, 8, 128), f32),
+            pltpu.VMEM((LINE, LINE, ROWS, 128), f32),
+            pltpu.VMEM((LINE, FULL, FULL), bf16),
+            pltpu.VMEM((LINE, FULL, ROWS), bf16),
+            pltpu.VMEM((ROWS, FULL), bf16),
+            pltpu.VMEM((COLS, FULL), bf16),
+            pltpu.VMEM((LINE, LINE, 16, ROWS), f32),
+            pltpu.VMEM((FULL, ROWS), bf16),
+            pltpu.VMEM((FULL, COLS), bf16),
+            pltpu.VMEM((FULL, FULL), bf16),
+            pltpu.VMEM((FULL, COLS), bf16),
+            pltpu.SemaphoreType.DMA((5, LINE)),
+            pltpu.SemaphoreType.DMA((LINE, LINE)),
+            pltpu.SemaphoreType.DMA((LINE * LINE - 1,)),
+            pltpu.SemaphoreType.DMA((LINE, LINE)),
+        ],
+        compiler_params=pltpu.CompilerParams(
+            collective_id=0, has_side_effects=True, vmem_limit_bytes=48 * 1024 * 1024
+        ),
+        cost_estimate=pl.CostEstimate(flops=13_000_000_000, bytes_accessed=8_000_000, transcendentals=0),
+    )(hamiltonian, row_ids, col_ids, counts)
 
 
 def shards(hamiltonian, row_ids, col_ids, counts):
@@ -115,4 +401,5 @@
         P(("sys", "row"), "col", None),
     )
     out_specs = P(("sys", "row"), "col")
-    return jax.shard_map(shards, mesh=mesh, in_specs=in_specs, out_specs=out_specs, check_vma=False)
+    small = mesh.shape["row"] == LINE and mesh.shape["col"] == LINE
+    return jax.shard_map(line_shards if small else shards, mesh=mesh, in_specs=in_specs, out_specs=out_specs, check_vma=False)

time: 265 us -> 68 us (0.26)
  blocking collectives: 123 us -> 0 us
  waiting for transfers between devices: 70.7 us -> 0 us
  Pallas kernels: 0 us -> 64.1 us
  local copies, waits for them, and re-layouts: 37.3 us -> 3.62 us
  between operations: 15.3 us -> 0.01 us
  matrix products: 11.1 us -> 0 us
  other arithmetic: 6.18 us -> 0 us
    all_gather x3 -> x0, blocking collectives: 93.1 us -> none  [the longest x1 33.8 us: shards(): lax.all_gather(counts, ('row', 'col'), axis=0, tiled=True)]
    all_gather x6 -> x0, waiting for transfers between devices: 69.4 us -> none  [the longest x4 42 us: multiply(): piece = lax.all_gather(right, 'row', axis=0, tiled=True)]
    pallas_call x0 -> x1, Pallas kernels: none -> 64.1 us  [line_shards(): pl.pallas_call(lines_kernel, out_shape=jax.ShapeDtypeStruct((ROWS, COLS),...]
    psum x1 -> x0, blocking collectives: 30.4 us -> none  [shards(): total = lax.psum(jnp.sum(energy * energy), ('row', 'col'))]
    reshape x10 -> x0, local copies, waits for them, and re-layouts: 22.4 us -> none  [the longest x8 18.7 us: multiply(): blocks = piece.reshape(tiles, tile_rows, CT, BLK)]
    dot_general x10 -> x0, matrix products: 11.1 us -> none  [the longest x4 4.76 us: multiply(): return jnp.dot(picked, moved, preferred_element_type=jnp.float32)]
    another operation x4 -> x0, local copies, waits for them, and re-layouts: 5.98 us -> none  [multiply(): left_blocks = left_full.reshape(tile_rows, grid_cols * CT, BLK)]
    convert_element_type x4 -> x0, local copies, waits for them, and re-layouts: 3.25 us -> none  [multiply(): moved = moved.astype(jnp.bfloat16).reshape(piece_rows, tile_cols)]
  transfers between devices with their start and end apart: 6 -> 0, of which waited for: 4 -> 0; matrix products, arithmetic and copies ran while one was open for 6% -> 0% of each run, Pallas kernels for 0% -> 0%
where the time goes in v1:
time: 68 us; the launch traced here: 67.8 us
  Pallas kernels  64.1 us (94%)
  local copies, waits for them, and re-layouts  3.62 us (5%)
    pallas_call x1, Pallas kernels, line_shards(): pl.pallas_call(lines_kernel, out_shape=jax.ShapeDtypeStruct((ROWS, COLS),...  64.1 us
    unnamed x9, local copies, waits for them, and re-layouts  3.62 us

profile of v1, /device:TPU:0, one launch (start us, length us, event | category | flops | bytes accessed | tf_op | source)
XLA Modules:
  0.0 67.8 jit_solution(582547085615091131)
XLA Ops:
  0.0 0.0 copy-start
  0.0 0.9 %copy-done = bf16[256,512]{1,0:T(8,128)(2,1)S(1)} copy-done((bf16[256,512]{1,0:T(8,128)(2,1)S(1)}, bf16[256,512]{1,0:T(8,128)(2,1)}, u32[]{:S(2)}) %copy-start) | copy-done | bytes 262168
  1.0 0.0 copy-start.1
  1.0 0.7 copy-done.1
  1.6 0.0 copy-start.2
  1.6 0.7 copy-done.2
  2.3 0.0 copy-start.3
  2.3 0.7 copy-done.3
  2.9 64.1 %shard_map.46 = bf16[256,512]{1,0:T(8,128)(2,1)S(1)} custom-call(bf16[256,512]{1,0:T(8,128)(2,1)S(1)} %copy-done, s32[1,1,4]{2,1,0:T(1,128)S(1)} %copy-done.1, s32[1,1,8]{2,1,0:T(1,128)S(1)} %copy-done.2, s32[1,1,2]{2,1,0:T(1,128)S(1)} %copy-done.3), custom_call_target="tpu_custom_call" | custom-call | flops 12999999488 | bytes 8000000 | tf_op jit(solution)/shard_map/pallas_call | solution.py:269
  67.1 0.7 %copy.6 = bf16[256,512]{1,0:T(8,128)(2,1)} copy(bf16[256,512]{1,0:T(8,128)(2,1)S(1)} %shard_map.46) | data formatting | bytes 524288
Async XLA Ops:
  0.0 0.9 %copy-start = (bf16[256,512]{1,0:T(8,128)(2,1)S(1)}, bf16[256,512]{1,0:T(8,128)(2,1)}, u32[]{:S(2)}) copy-start(bf16[256,512]{1,0:T(8,128)(2,1)} %h_ref.1) | copy-start | bytes 786436
  1.0 0.7 copy-start.1
  1.6 0.7 copy-start.2
  2.3 0.7 copy-start.3

commit v2 on v0

--- a/solution.py
+++ b/solution.py
@@ -1,6 +1,8 @@
 import jax
 import jax.numpy as jnp
 from jax import lax
+from jax.experimental import pallas as pl
+from jax.experimental.pallas import tpu as pltpu
 from jax.sharding import PartitionSpec as P
 
 BLK = 64
@@ -8,6 +10,305 @@
 RT = 4
 CT = 8
 NS_STEPS = 2
+
+LINE = 4
+ROWS = RT * BLK
+COLS = CT * BLK
+FULL = LINE * ROWS
+PARTS = 2
+PART = ROWS // PARTS
+MESH_IDS = pl.DeviceIdType.MESH
+
+
+def onehot(found):
+    return jnp.where(found, 1.0, 0.0).astype(jnp.bfloat16)
+
+
+def dot(a, b):
+    return jnp.dot(a, b, preferred_element_type=jnp.float32)
+
+
+def lines_kernel(
+    h_any, rid_any, cid_any, cnt_any, o_ref,
+    h_ref, rid, cid, cnt, tiles, meta, short_ids, ids, left, right, picked, select, masks, half, whole, left2, square2,
+    send, recv, meta_send, meta_recv, load,
+):
+    loads = [
+        pltpu.make_async_copy(src, dst, load.at[n])
+        for n, (src, dst) in enumerate(((rid_any, rid), (cid_any, cid), (cnt_any, cnt), (h_any, h_ref)))
+    ]
+    for item in loads:
+        item.start()
+    k = lax.axis_index("row")
+    z = lax.axis_index("col")
+    ks = k + 1 - 2 * (k % 2)
+    kx = (k + 2) % LINE
+    kxs = (ks + 2) % LINE
+    barrier = pltpu.get_barrier_semaphore()
+    peers = [((k + a) % LINE, z) for a in range(1, LINE)] + [(k, (z + a) % LINE) for a in range(1, LINE)]
+    for row, col in peers:
+        pl.semaphore_signal(barrier, inc=1, device_id={"row": row, "col": col}, device_id_type=MESH_IDS)
+    for item in loads[:3]:
+        item.wait()
+    live_rows = cnt[0, 0, 0]
+    live_cols = cnt[0, 0, 1]
+
+    lane1 = lax.broadcasted_iota(jnp.int32, (1, COLS), 1)
+    block1 = lane1 // BLK
+    within = lane1 % BLK
+    row_full = jnp.full((1, COLS), -1, jnp.int32)
+    for r in range(RT):
+        row_full = jnp.where((block1 == r) & (r < live_rows), rid[0, 0, r] * BLK + within, row_full)
+    col_mask = jnp.zeros((1, COLS), jnp.int32)
+    col_full = jnp.full((1, COLS), -1, jnp.int32)
+    for c in range(CT):
+        alive = c < live_cols
+        col_mask = jnp.where((block1 == cid[0, 0, c]) & alive, 1, col_mask)
+        col_full = jnp.where((block1 == c) & alive, cid[0, 0, c] * BLK + within, col_full)
+    own_meta = meta.at[z, k]
+    own_meta[0:1, :] = row_full[:, 0:128]
+    own_meta[1:2, :] = row_full[:, 128:256]
+    for q in range(4):
+        own_meta[2 + q:3 + q, :] = col_mask[:, q * 128:(q + 1) * 128]
+    short = jnp.where(lane1[:, 0:128] == RT, live_rows, -1)
+    for r in range(RT):
+        short = jnp.where((lane1[:, 0:128] == r) & (r < live_rows), rid[0, 0, r], short)
+    own_meta[6:7, :] = short
+    own_meta[7:8, :] = short
+    lane = lax.broadcasted_iota(jnp.int32, (BLK, COLS), 1)
+    sub = lax.broadcasted_iota(jnp.int32, (BLK, COLS), 0)
+    for c in range(CT):
+        offset = jnp.where(c < live_cols, cid[0, 0, c] * BLK, -COLS)
+        select[pl.ds(c * BLK, BLK), 0:COLS] = onehot(sub + offset == lane)
+    loads[3].wait()
+    natural = dot(h_ref[...], select[:, 0:COLS])
+    for r in range(RT):
+        part = natural[r * BLK:(r + 1) * BLK] * jnp.where(r < live_rows, 1.0, 0.0)
+        tiles[z, pl.ds(pl.multiple_of(k * ROWS + r * BLK, BLK), BLK), :] = part.astype(jnp.bfloat16)
+    pl.semaphore_wait(barrier, len(peers))
+
+    def piece(kk, m, part):
+        return tiles.at[m, pl.ds(pl.multiple_of(kk * ROWS + part * PART, PART), PART), :]
+
+    def copy(kind, kk, m, part, row, col):
+        return pltpu.make_async_remote_copy(
+            src_ref=piece(kk, m, part), dst_ref=piece(kk, m, part),
+            send_sem=send.at[kind, m, part], recv_sem=recv.at[kk, m, part],
+            device_id={"row": row, "col": col}, device_id_type=MESH_IDS,
+        )
+
+    def row_ids_copy(n, owner, row):
+        return pltpu.make_async_remote_copy(
+            src_ref=meta.at[z, owner], dst_ref=meta.at[z, owner],
+            send_sem=meta_send.at[n], recv_sem=meta_recv.at[0, owner],
+            device_id={"row": row, "col": z}, device_id_type=MESH_IDS,
+        )
+
+    def line_ids_copy(n, owner, col):
+        return pltpu.make_async_remote_copy(
+            src_ref=meta.at[owner], dst_ref=meta.at[owner],
+            send_sem=meta_send.at[n], recv_sem=meta_recv.at[1, owner],
+            device_id={"row": k, "col": col}, device_id_type=MESH_IDS,
+        )
+
+    def line_copies(m, part, act):
+        @pl.when((m <= z) & (z < LINE - 1))
+        def _():
+            act(copy(0, k, m, part, k, z + 1))
+
+        @pl.when((m >= z) & (z > 0))
+        def _():
+            act(copy(1, k, m, part, k, z - 1))
+
+        act(copy(2, k, m, part, kx, z))
+        act(copy(3, k, m, part, ks, z))
+
+    def start(c):
+        c.start()
+
+    def finish(c):
+        c.wait_send()
+
+    def arrived(kk, m, part):
+        copy(0, kk, m, part, ks, z).wait_recv()
+
+    high = z // 2
+    near = z * (1 - high) + (LINE - 1 - z) * high
+
+    def panel_at(t):
+        later = t // 2
+        m = 2 * later + (t + near * (1 - later)) % 2
+        return m * (1 - high) + (LINE - 1 - m) * high
+
+    for n, (row, _) in enumerate(peers[:3]):
+        row_ids_copy(n, k, row).start()
+    for part in range(PARTS):
+        line_copies(z, part, start)
+    for row, _ in peers[:3]:
+        row_ids_copy(0, row, row).wait_recv()
+    for n, (_, col) in enumerate(peers[3:]):
+        line_ids_copy(3 + n, z, col).start()
+    for _, col in peers[3:]:
+        line_ids_copy(3, col, col).wait_recv()
+    for m in range(LINE):
+        for kk in range(LINE):
+            short_ids[pl.ds(m * LINE + kk, 1), :] = meta[m, kk, 6:7, :]
+    spell = pltpu.make_async_copy(short_ids, ids, load.at[4])
+    spell.start()
+    spell.wait()
+
+    def lane_ids(kk, m):
+        return jnp.concatenate([meta[m, kk, 0:1, :], meta[m, kk, 1:2, :]], axis=1)
+
+    def natural_mask(kk, m):
+        return jnp.concatenate([meta[m, kk, 2 + q:3 + q, :] for q in range(4)], axis=1).astype(jnp.float32)
+
+    def pick_rows(kk, to, of):
+        blocks = []
+        for r in range(RT):
+            want = ids[to * LINE + kk, r]
+            block = jnp.zeros((BLK, ROWS), jnp.bfloat16)
+            for a in range(RT):
+                same = (ids[of * LINE + kk, a] == want) & (want >= 0)
+                block = jnp.where(same, picked[pl.ds(kk * ROWS + a * BLK, BLK), :], block)
+            blocks.append(block)
+        return jnp.concatenate(blocks, axis=0)
+
+    sub_wide = lax.broadcasted_iota(jnp.int32, (COLS, ROWS), 0)
+
+    def col_select(m, to):
+        return onehot(sub_wide == lane_ids(m, to))
+
+    def wide_slice(index):
+        return pl.ds(pl.multiple_of(index * ROWS, ROWS), ROWS)
+
+    def stage(t, carry):
+        for now, then in ((0, 1), (0, 2), (1, 3)):
+            @pl.when(t == now)
+            def _(then=then):
+                m1 = panel_at(then)
+                for part in range(PARTS):
+                    arrived(k, m1, part)
+                    line_copies(m1, part, start)
+
+        m = panel_at(t)
+        for part in range(PARTS):
+            arrived(kx, m, part)
+            copy(4, kx, m, part, ks, z).start()
+        for to in range(LINE):
+            select[:, pl.ds(to * ROWS, ROWS)] = col_select(m, to)
+        for part in range(PARTS):
+            arrived(ks, m, part)
+            arrived(kxs, m, part)
+
+        mask = jnp.concatenate(
+            [natural_mask(kk, m) for kk in range(LINE)] + [jnp.zeros((12, COLS), jnp.float32)], axis=0
+        )
+        masks[m] = dot(mask.astype(jnp.bfloat16), select[:, wide_slice(z)])
+        for to in range(LINE):
+            picked[0:FULL, :] = dot(tiles[m], select[:, pl.ds(to * ROWS, ROWS)]).astype(jnp.bfloat16)
+
+            @pl.when(z == to)
+            def _():
+                right[m] = picked[0:FULL, :]
+
+            for kk in range(LINE):
+                left[to, pl.ds(kk * ROWS, ROWS), wide_slice(m)] = pick_rows(kk, to, m)
+        values = tiles[m].astype(jnp.float32)
+        return carry + jnp.sum(values * values, axis=0, keepdims=True)
+
+    total = lax.fori_loop(0, LINE, stage, jnp.zeros((1, COLS), jnp.float32))
+
+    total = jnp.sum(total, axis=1, keepdims=True)
+    count = jnp.int32(0)
+    for a in range(LINE):
+        for b in range(LINE):
+            count += ids[a * LINE + b, RT]
+    count = jnp.full((1, 1), count * BLK, jnp.int32).astype(jnp.float32)
+    scale = 2.0 * jnp.sqrt(LINE * total / count + 1e-06)
+    lin = 1.5 / scale
+    cub = 0.5 / scale / scale / scale
+
+    def spread(rows):
+        return jnp.concatenate([jnp.broadcast_to(row, (ROWS, row.shape[1])) for row in rows], axis=0)
+
+    def other(d, carry):
+        m = (z + d) % LINE
+        mask = spread([masks[m, kk:kk + 1, :] for kk in range(LINE)])
+        half[...] = (dot(left[m], right[m]) * mask).astype(jnp.bfloat16)
+        part = dot(left[m], half[...]) * mask
+        picked[0:FULL, :] = (lin * right[m].astype(jnp.float32) - cub * part).astype(jnp.bfloat16)
+        for kk in range(LINE):
+            left2[pl.ds(kk * ROWS, ROWS), wide_slice(m)] = pick_rows(kk, z, m)
+        return carry
+
+    lax.fori_loop(1, LINE, other, 0)
+
+    mask = spread([natural_mask(kk, z) for kk in range(LINE)])
+    square2[...] = (dot(left[z], tiles[z]) * mask).astype(jnp.bfloat16)
+    select[:, 0:ROWS] = col_select(z, z)
+    part = dot(left[z], square2[...]) * mask
+    whole[...] = (lin * tiles[z].astype(jnp.float32) - cub * part).astype(jnp.bfloat16)
+    left2[:, wide_slice(z)] = dot(whole[...], select[:, 0:ROWS]).astype(jnp.bfloat16)
+    square2[...] = (dot(left2[...], whole[...]) * mask).astype(jnp.bfloat16)
+    cube = dot(left2[wide_slice(k), :], square2[...]) * natural_mask(k, z)
+    update = 1.5 * whole[wide_slice(k), :].astype(jnp.float32) - 0.5 * cube
+    final = (update * scale).astype(jnp.bfloat16)
+    back = onehot(lax.broadcasted_iota(jnp.int32, (COLS, COLS), 0) == col_full)
+    o_ref[...] = dot(final, back).astype(jnp.bfloat16)
+
+    for n, (row, _) in enumerate(peers[:3]):
+        row_ids_copy(n, k, row).wait_send()
+    for n, (_, col) in enumerate(peers[3:]):
+        line_ids_copy(3 + n, z, col).wait_send()
+
+    def drain(m, carry):
+        for part in range(PARTS):
+            line_copies(m, part, finish)
+            copy(4, kx, m, part, ks, z).wait_send()
+        return carry
+
+    lax.fori_loop(0, LINE, drain, 0)
+
+
+def line_shards(hamiltonian, row_ids, col_ids, counts):
+    hbm = pl.BlockSpec(memory_space=pl.ANY)
+    vmem = pl.BlockSpec(memory_space=pltpu.VMEM)
+    bf16, f32 = jnp.bfloat16, jnp.float32
+    return pl.pallas_call(
+        lines_kernel,
+        out_shape=jax.ShapeDtypeStruct((ROWS, COLS), bf16),
+        in_specs=[hbm, hbm, hbm, hbm],
+        out_specs=vmem,
+        scratch_shapes=[
+            pltpu.VMEM((ROWS, COLS), bf16),
+            pltpu.SMEM(row_ids.shape, jnp.int32),
+            pltpu.SMEM(col_ids.shape, jnp.int32),
+            pltpu.SMEM(counts.shape, jnp.int32),
+            pltpu.VMEM((LINE, FULL, COLS), bf16),
+            pltpu.VMEM((LINE, LINE, 8, 128), jnp.int32),
+            pltpu.VMEM((LINE * LINE, 128), jnp.int32),
+            pltpu.SMEM((LINE * LINE, 128), jnp.int32),
+            pltpu.VMEM((LINE, FULL, FULL), bf16),
+            pltpu.VMEM((LINE, FULL, ROWS), bf16),
+            pltpu.VMEM((FULL, ROWS), bf16),
+            pltpu.VMEM((COLS, FULL), bf16),
+            pltpu.VMEM((LINE, 16, ROWS), f32),
+            pltpu.VMEM((FULL, ROWS), bf16),
+            pltpu.VMEM((FULL, COLS), bf16),
+            pltpu.VMEM((FULL, FULL), bf16),
+            pltpu.VMEM((FULL, COLS), bf16),
+            pltpu.SemaphoreType.DMA((5, LINE, PARTS)),
+            pltpu.SemaphoreType.DMA((LINE, LINE, PARTS)),
+            pltpu.SemaphoreType.DMA((6,)),
+            pltpu.SemaphoreType.DMA((2, LINE)),
+            pltpu.SemaphoreType.DMA((5,)),
+        ],
+        compiler_params=pltpu.CompilerParams(
+            collective_id=0, has_side_effects=True, vmem_limit_bytes=48 * 1024 * 1024
+        ),
+        cost_estimate=pl.CostEstimate(flops=13_000_000_000, bytes_accessed=8_000_000, transcendentals=0),
+    )(hamiltonian, row_ids, col_ids, counts)
 
 
 def shards(hamiltonian, row_ids, col_ids, counts):
@@ -115,4 +416,5 @@
         P(("sys", "row"), "col", None),
     )
     out_specs = P(("sys", "row"), "col")
-    return jax.shard_map(shards, mesh=mesh, in_specs=in_specs, out_specs=out_specs, check_vma=False)
+    small = mesh.shape["row"] == LINE and mesh.shape["col"] == LINE
+    return jax.shard_map(line_shards if small else shards, mesh=mesh, in_specs=in_specs, out_specs=out_specs, check_vma=False)

time: 265 us -> 56.8 us (0.21)
  blocking collectives: 123 us -> 0 us
  waiting for transfers between devices: 70.7 us -> 0 us
  Pallas kernels: 0 us -> 52.5 us
  local copies, waits for them, and re-layouts: 37.3 us -> 3.62 us
  between operations: 15.3 us -> 0.01 us
  matrix products: 11.1 us -> 0 us
  other arithmetic: 6.18 us -> 0 us
    all_gather x3 -> x0, blocking collectives: 93.1 us -> none  [the longest x1 33.8 us: shards(): lax.all_gather(counts, ('row', 'col'), axis=0, tiled=True)]
    all_gather x6 -> x0, waiting for transfers between devices: 69.4 us -> none  [the longest x4 42 us: multiply(): piece = lax.all_gather(right, 'row', axis=0, tiled=True)]
    pallas_call x0 -> x1, Pallas kernels: none -> 52.5 us  [line_shards(): pl.pallas_call(lines_kernel, out_shape=jax.ShapeDtypeStruct((ROWS, COLS),...]
    psum x1 -> x0, blocking collectives: 30.4 us -> none  [shards(): total = lax.psum(jnp.sum(energy * energy), ('row', 'col'))]
    reshape x10 -> x0, local copies, waits for them, and re-layouts: 22.4 us -> none  [the longest x8 18.7 us: multiply(): blocks = piece.reshape(tiles, tile_rows, CT, BLK)]
    dot_general x10 -> x0, matrix products: 11.1 us -> none  [the longest x4 4.76 us: multiply(): return jnp.dot(picked, moved, preferred_element_type=jnp.float32)]
    another operation x4 -> x0, local copies, waits for them, and re-layouts: 5.98 us -> none  [multiply(): left_blocks = left_full.reshape(tile_rows, grid_cols * CT, BLK)]
    convert_element_type x4 -> x0, local copies, waits for them, and re-layouts: 3.25 us -> none  [multiply(): moved = moved.astype(jnp.bfloat16).reshape(piece_rows, tile_cols)]
  transfers between devices with their start and end apart: 6 -> 0, of which waited for: 4 -> 0; matrix products, arithmetic and copies ran while one was open for 6% -> 0% of each run, Pallas kernels for 0% -> 0%
where the time goes in v2:
time: 56.8 us; the launch traced here: 56.2 us
  Pallas kernels  52.5 us (92%)
  local copies, waits for them, and re-layouts  3.62 us (6%)
    pallas_call x1, Pallas kernels, line_shards(): pl.pallas_call(lines_kernel, out_shape=jax.ShapeDtypeStruct((ROWS, COLS),...  52.5 us
    unnamed x9, local copies, waits for them, and re-layouts  3.62 us

profile of v2, /device:TPU:0, one launch (start us, length us, event | category | flops | bytes accessed | tf_op | source)
XLA Modules:
  0.0 56.2 jit_solution(10298464984729794253)
XLA Ops:
  0.0 0.0 copy-start
  0.0 0.9 %copy-done = bf16[256,512]{1,0:T(8,128)(2,1)S(1)} copy-done((bf16[256,512]{1,0:T(8,128)(2,1)S(1)}, bf16[256,512]{1,0:T(8,128)(2,1)}, u32[]{:S(2)}) %copy-start) | copy-done | bytes 262168
  1.0 0.0 copy-start.1
  1.0 0.7 %copy-done.1 = s32[1,1,4]{2,1,0:T(1,128)S(1)} copy-done((s32[1,1,4]{2,1,0:T(1,128)S(1)}, s32[1,1,4]{2,1,0:T(1,128)}, u32[]{:S(2)}) %copy-start.1) | copy-done | bytes 40
  1.6 0.0 copy-start.2
  1.6 0.7 %copy-done.2 = s32[1,1,8]{2,1,0:T(1,128)S(1)} copy-done((s32[1,1,8]{2,1,0:T(1,128)S(1)}, s32[1,1,8]{2,1,0:T(1,128)}, u32[]{:S(2)}) %copy-start.2) | copy-done | bytes 56
  2.3 0.0 copy-start.3
  2.3 0.7 %copy-done.3 = s32[1,1,2]{2,1,0:T(1,128)S(1)} copy-done((s32[1,1,2]{2,1,0:T(1,128)S(1)}, s32[1,1,2]{2,1,0:T(1,128)}, u32[]{:S(2)}) %copy-start.3) | copy-done | bytes 32
  2.9 52.5 %shard_map.46 = bf16[256,512]{1,0:T(8,128)(2,1)S(1)} custom-call(bf16[256,512]{1,0:T(8,128)(2,1)S(1)} %copy-done, s32[1,1,4]{2,1,0:T(1,128)S(1)} %copy-done.1, s32[1,1,8]{2,1,0:T(1,128)S(1)} %copy-done.2, s32[1,1,2]{2,1,0:T(1,128)S(1)} %copy-done.3), custom_call_target="tpu_custom_call" | custom-call | flops 12999999488 | bytes 8000000 | tf_op jit(solution)/shard_map/pallas_call | solution.py:278
  55.5 0.7 %copy.6 = bf16[256,512]{1,0:T(8,128)(2,1)} copy(bf16[256,512]{1,0:T(8,128)(2,1)S(1)} %shard_map.46) | data formatting | bytes 524288
Async XLA Ops:
  0.0 0.9 %copy-start = (bf16[256,512]{1,0:T(8,128)(2,1)S(1)}, bf16[256,512]{1,0:T(8,128)(2,1)}, u32[]{:S(2)}) copy-start(bf16[256,512]{1,0:T(8,128)(2,1)} %h_any.1) | copy-start | bytes 786436
  1.0 0.7 %copy-start.1 = (s32[1,1,4]{2,1,0:T(1,128)S(1)}, s32[1,1,4]{2,1,0:T(1,128)}, u32[]{:S(2)}) copy-start(s32[1,1,4]{2,1,0:T(1,128)} %rid_any.1) | copy-start | bytes 52
  1.6 0.7 %copy-start.2 = (s32[1,1,8]{2,1,0:T(1,128)S(1)}, s32[1,1,8]{2,1,0:T(1,128)}, u32[]{:S(2)}) copy-start(s32[1,1,8]{2,1,0:T(1,128)} %cid_any.1) | copy-start | bytes 100
  2.3 0.7 %copy-start.3 = (s32[1,1,2]{2,1,0:T(1,128)S(1)}, s32[1,1,2]{2,1,0:T(1,128)}, u32[]{:S(2)}) copy-start(s32[1,1,2]{2,1,0:T(1,128)} %cnt_any.1) | copy-start | bytes 28

commit v3 on v2

--- a/solution.py
+++ b/solution.py
@@ -30,7 +30,7 @@
 
 def lines_kernel(
     h_any, rid_any, cid_any, cnt_any, o_ref,
-    h_ref, rid, cid, cnt, tiles, meta, short_ids, ids, left, right, picked, select, masks, half, whole, left2, square2,
+    h_ref, rid, cid, cnt, tiles, meta, short_ids, ids, left, right, wide, picked, select, masks, half, whole, left2, square2,
     send, recv, meta_send, meta_recv, load,
 ):
     loads = [
@@ -163,14 +163,14 @@
     def natural_mask(kk, m):
         return jnp.concatenate([meta[m, kk, 2 + q:3 + q, :] for q in range(4)], axis=1).astype(jnp.float32)
 
-    def pick_rows(kk, to, of):
+    def pick_rows(kk, to, of, block_at):
         blocks = []
         for r in range(RT):
             want = ids[to * LINE + kk, r]
             block = jnp.zeros((BLK, ROWS), jnp.bfloat16)
             for a in range(RT):
                 same = (ids[of * LINE + kk, a] == want) & (want >= 0)
-                block = jnp.where(same, picked[pl.ds(kk * ROWS + a * BLK, BLK), :], block)
+                block = jnp.where(same, block_at(a), block)
             blocks.append(block)
         return jnp.concatenate(blocks, axis=0)
 
@@ -205,15 +205,16 @@
             [natural_mask(kk, m) for kk in range(LINE)] + [jnp.zeros((12, COLS), jnp.float32)], axis=0
         )
         masks[m] = dot(mask.astype(jnp.bfloat16), select[:, wide_slice(z)])
-        for to in range(LINE):
-            picked[0:FULL, :] = dot(tiles[m], select[:, pl.ds(to * ROWS, ROWS)]).astype(jnp.bfloat16)
-
-            @pl.when(z == to)
-            def _():
-                right[m] = picked[0:FULL, :]
-
-            for kk in range(LINE):
-                left[to, pl.ds(kk * ROWS, ROWS), wide_slice(m)] = pick_rows(kk, to, m)
+        def rows_of(kk, carry):
+            wide[...] = dot(tiles[m, wide_slice(kk), :], select[...]).astype(jnp.bfloat16)
+            right[m, wide_slice(kk), :] = wide[:, wide_slice(z)]
+            for to in range(LINE):
+                left[to, wide_slice(kk), wide_slice(m)] = pick_rows(
+                    kk, to, m, lambda a, to=to: wide[pl.ds(a * BLK, BLK), pl.ds(to * ROWS, ROWS)]
+                )
+            return carry
+
+        lax.fori_loop(0, LINE, rows_of, 0)
         values = tiles[m].astype(jnp.float32)
         return carry + jnp.sum(values * values, axis=0, keepdims=True)
 
@@ -239,7 +240,9 @@
         part = dot(left[m], half[...]) * mask
         picked[0:FULL, :] = (lin * right[m].astype(jnp.float32) - cub * part).astype(jnp.bfloat16)
         for kk in range(LINE):
-            left2[pl.ds(kk * ROWS, ROWS), wide_slice(m)] = pick_rows(kk, z, m)
+            left2[pl.ds(kk * ROWS, ROWS), wide_slice(m)] = pick_rows(
+                kk, z, m, lambda a, kk=kk: picked[pl.ds(kk * ROWS + a * BLK, BLK), :]
+            )
         return carry
 
     lax.fori_loop(1, LINE, other, 0)
@@ -291,6 +294,7 @@
             pltpu.SMEM((LINE * LINE, 128), jnp.int32),
             pltpu.VMEM((LINE, FULL, FULL), bf16),
             pltpu.VMEM((LINE, FULL, ROWS), bf16),
+            pltpu.VMEM((ROWS, FULL), bf16),
             pltpu.VMEM((FULL, ROWS), bf16),
             pltpu.VMEM((COLS, FULL), bf16),
             pltpu.VMEM((LINE, 16, ROWS), f32),

time: 56.8 us -> 53.8 us (0.947)
  Pallas kernels: 52.5 us -> 49.2 us
    pallas_call x1, Pallas kernels: 52.5 us -> 49.2 us  [line_shards(): pl.pallas_call(lines_kernel, out_shape=jax.ShapeDtypeStruct((ROWS, COLS),...]
where the time goes in v3:
time: 53.8 us; the launch traced here: 52.8 us
  Pallas kernels  49.2 us (91%)
  local copies, waits for them, and re-layouts  3.62 us (7%)
    pallas_call x1, Pallas kernels, line_shards(): pl.pallas_call(lines_kernel, out_shape=jax.ShapeDtypeStruct((ROWS, COLS),...  49.2 us
    unnamed x9, local copies, waits for them, and re-layouts  3.62 us

profile of v3, /device:TPU:0, one launch (start us, length us, event | category | flops | bytes accessed | tf_op | source)
XLA Modules:
  0.0 52.8 jit_solution(5993367755537286979)
XLA Ops:
  0.0 0.0 copy-start
  0.0 0.9 %copy-done = bf16[256,512]{1,0:T(8,128)(2,1)S(1)} copy-done((bf16[256,512]{1,0:T(8,128)(2,1)S(1)}, bf16[256,512]{1,0:T(8,128)(2,1)}, u32[]{:S(2)}) %copy-start) | copy-done | bytes 262168
  1.0 0.0 copy-start.1
  1.0 0.7 %copy-done.1 = s32[1,1,4]{2,1,0:T(1,128)S(1)} copy-done((s32[1,1,4]{2,1,0:T(1,128)S(1)}, s32[1,1,4]{2,1,0:T(1,128)}, u32[]{:S(2)}) %copy-start.1) | copy-done | bytes 40
  1.6 0.0 copy-start.2
  1.6 0.7 %copy-done.2 = s32[1,1,8]{2,1,0:T(1,128)S(1)} copy-done((s32[1,1,8]{2,1,0:T(1,128)S(1)}, s32[1,1,8]{2,1,0:T(1,128)}, u32[]{:S(2)}) %copy-start.2) | copy-done | bytes 56
  2.3 0.0 copy-start.3
  2.3 0.7 %copy-done.3 = s32[1,1,2]{2,1,0:T(1,128)S(1)} copy-done((s32[1,1,2]{2,1,0:T(1,128)S(1)}, s32[1,1,2]{2,1,0:T(1,128)}, u32[]{:S(2)}) %copy-start.3) | copy-done | bytes 32
  2.9 49.2 %shard_map.46 = bf16[256,512]{1,0:T(8,128)(2,1)S(1)} custom-call(bf16[256,512]{1,0:T(8,128)(2,1)S(1)} %copy-done, s32[1,1,4]{2,1,0:T(1,128)S(1)} %copy-done.1, s32[1,1,8]{2,1,0:T(1,128)S(1)} %copy-done.2, s32[1,1,2]{2,1,0:T(1,128)S(1)} %copy-done.3), custom_call_target="tpu_custom_call" | custom-call | flops 12999999488 | bytes 8000000 | tf_op jit(solution)/shard_map/pallas_call | solution.py:281
  52.1 0.7 %copy.6 = bf16[256,512]{1,0:T(8,128)(2,1)} copy(bf16[256,512]{1,0:T(8,128)(2,1)S(1)} %shard_map.46) | data formatting | bytes 524288
Async XLA Ops:
  0.0 0.9 %copy-start = (bf16[256,512]{1,0:T(8,128)(2,1)S(1)}, bf16[256,512]{1,0:T(8,128)(2,1)}, u32[]{:S(2)}) copy-start(bf16[256,512]{1,0:T(8,128)(2,1)} %h_any.1) | copy-start | bytes 786436
  1.0 0.7 %copy-start.1 = (s32[1,1,4]{2,1,0:T(1,128)S(1)}, s32[1,1,4]{2,1,0:T(1,128)}, u32[]{:S(2)}) copy-start(s32[1,1,4]{2,1,0:T(1,128)} %rid_any.1) | copy-start | bytes 52
  1.6 0.7 %copy-start.2 = (s32[1,1,8]{2,1,0:T(1,128)S(1)}, s32[1,1,8]{2,1,0:T(1,128)}, u32[]{:S(2)}) copy-start(s32[1,1,8]{2,1,0:T(1,128)} %cid_any.1) | copy-start | bytes 100
  2.3 0.7 %copy-start.3 = (s32[1,1,2]{2,1,0:T(1,128)S(1)}, s32[1,1,2]{2,1,0:T(1,128)}, u32[]{:S(2)}) copy-start(s32[1,1,2]{2,1,0:T(1,128)} %cnt_any.1) | copy-start | bytes 28
